TPU v7x, 256 devices: a whole 4x4x8 slice. The times are simulated.
256 devices in a mesh: ctx: 16 (over y_hi, x, core), tp: 16 (over y_lo, z).
Axes of the slice: x: 4, y: 4 (y_hi: 2, y_lo: 2; y = y_hi * 2 + y_lo), z: 8, core: 2. Of those that a mesh axis runs over, the one named last changes fastest.
Arguments:
- q_nope: bfloat16 [4096, 16384], P('ctx', 'tp'), may hold values from -6 to 6
- q_rope: bfloat16 [4096, 8192], P('ctx', 'tp'), may hold values from -6 to 6
- latent: bfloat16 [32768, 512], P('ctx'), may hold values from -6 to 6
- key_rope: bfloat16 [512, 4096], P('ctx'), may hold values from -6 to 6
- w_uk: bfloat16 [128, 128, 512], P('tp'), may hold values from -0.5 to 0.5
- w_uv: bfloat16 [128, 512, 128], P('tp'), may hold values from -0.25 to 0.25
- w_out: bfloat16 [16384, 7168], P('tp', 'ctx'), may hold values from -0.046875 to 0.046875
- block_lists: int32 [64, 32], P('ctx'), may hold values from 0 to 511, as said below
Outputs:
- attended: bfloat16 [4096, 7168], P('ctx', 'tp')
Inputs may be any that keep to these rules, and one draw needn't show every extreme that they name: `block_lists`: each row lists 32 distinct blocks, none after the block of its own query block. Over the 4 rows of one ctx index, at most 6 distinct listed blocks lie among any one ctx index's 32 blocks of the cache, and exactly 6 among the first one's, the same ones in each of these rows, block 0 among them.
All inputs are finite; a program needn't handle non-finite values.
Results may differ from a plain program's by a relative error of at most 0.024.
Values may be sent and summed in bfloat16 or wider, within the bound.
A program may use at most 128 MiB of HBM per device.

v0:
```python
import functools
import math

import jax
import jax.numpy as jnp
from jax import lax
from jax.experimental import pallas as pl
from jax.experimental.pallas import tpu as pltpu
from jax.sharding import PartitionSpec as P

CAP = 6
N_CTX = 16
N_Z = 8
MESH = pl.DeviceIdType.MESH
bf16 = jnp.bfloat16
f32 = jnp.float32
VMEM_LIMIT = 60 * 1024 * 1024

mscale_sq = (0.1 * math.log(40.0) + 1.0) ** 2


RANKS = [(0, 0), (1, 0), (3, 0), (0, 1), (1, 1), (3, 1), (2, 0), (2, 1)]
N_DIRECT = 8


def shifted(me, dx, dy, dk):
    y, x, core = lax.div(me, 8), lax.rem(lax.div(me, 2), 4), lax.rem(me, 2)
    return lax.rem(y + dy, 2) * 8 + lax.rem(x + dx, 4) * 2 + lax.rem(core + dk, 2)


def owner_of(me, rank):
    dx, dy = RANKS[rank // 2]
    return shifted(me, dx, dy, rank % 2)


def asker_of(me, rank):
    dx, dy = RANKS[rank // 2]
    return shifted(me, (4 - dx) % 4, dy, rank % 2)


def rank_of(owner, me):
    dy = ((owner >> 3) - (me >> 3)) & 1
    dx = ((owner >> 1) - (me >> 1)) & 3
    rank = jnp.zeros_like(owner)
    for i, (x, y) in enumerate(RANKS):
        rank = jnp.where((dx == x) & (dy == y), 2 * i, rank)
    return rank + ((owner - me) & 1)


def sum_lanes(values):
    return jnp.sum(values, axis=1, keepdims=True)


def layer_kernel(
    lists,
    latent,
    rope_in,
    q_nope_in,
    q_rope_in,
    w_uk_in,
    w_uv_in,
    w_out,
    out,
    q_nope,
    q_rope,
    w_uk,
    w_uv,
    load_sems,
    rope,
    offsets,
    table,
    picked,
    got,
    asked,
    direct,
    shared,
    ropes,
    far_ropes,
    kv,
    rp,
    ask_send,
    ask_recv,
    ask_local,
    own_sems,
    ctx_send,
    ctx_recv,
    ring_send,
    ring_recv,
    qbuf,
    kbuf,
    heads_out,
    head_send,
    head_recv,
    w_buf,
    w_send,
    w_recv,
    part,
    sent,
    arrived,
    sum_send,
    sum_recv,
    last_sent,
    last_got,
    last_send,
    last_recv,
):
    me = lax.axis_index("ctx")
    t = lax.axis_index("tp")
    z = lax.rem(t, N_Z)
    y_lo = lax.div(t, N_Z)
    y_hi = lax.div(me, 8)
    x_core = lax.rem(me, 8)
    base = t - z
    right = base + lax.rem(z + 1, N_Z)
    left = base + lax.rem(z + N_Z - 1, N_Z)
    opposite = shifted(me, 0, 1, 0)
    other_core = shifted(me, 0, 0, 1)
    x_next = (shifted(me, 1, 0, 0), shifted(me, 3, 0, 0))
    home = y_hi * N_Z + z
    blk = 16 * latent.shape[1]
    half_blk = blk // 2
    block_groups = blk // 16
    share_groups = CAP * block_groups // N_Z
    heads, dn, dl = w_uk.shape
    dv = w_uv.shape[2]
    dr = q_rope.shape[1] // heads
    steps, blocks = lists.shape
    keys = blocks * blk
    queries = q_nope.shape[0]
    width = w_out.shape[0]
    half_width = width // 2

    barrier = pltpu.get_barrier_semaphore()
    for rank in range(1, N_CTX):
        pl.semaphore_signal(
            barrier, inc=1, device_id={"ctx": owner_of(me, rank)}, device_id_type=MESH
        )
    across = lax.rem(t + N_Z, 2 * N_Z)
    for peer in (left, right, across):
        pl.semaphore_signal(barrier, inc=1, device_id={"tp": peer}, device_id_type=MESH)
    pl.semaphore_signal(
        barrier, inc=1, device_id={"ctx": opposite, "tp": across}, device_id_type=MESH
    )

    own_w = pltpu.make_async_copy(w_out, w_buf.at[x_core], own_sems.at[2])
    own_w.start()
    loads = [
        pltpu.make_async_copy(src, dst, load_sems.at[i])
        for i, (src, dst) in enumerate(
            ((q_nope_in, q_nope), (q_rope_in, q_rope), (w_uk_in, w_uk), (w_uv_in, w_uv))
        )
    ]
    for copy in loads:
        copy.start()


    per_owner = latent.shape[0]
    total_blocks = N_CTX * per_owner
    ids = lax.broadcasted_iota(jnp.int32, (8, total_blocks), 1)
    listed = jnp.zeros((8, total_blocks), jnp.int32)
    for qb in range(steps):
        for j in range(blocks):
            listed = jnp.where(ids == lists[qb, j], 1, listed)
    place_of = listed
    shift = 1
    while shift < per_owner:
        moved = pltpu.roll(place_of, shift, 1)
        place_of = place_of + jnp.where((ids & (per_owner - 1)) >= shift, moved, 0)
        shift *= 2
    place_of = place_of - 1

    owner_row = lax.broadcasted_iota(jnp.int32, (N_CTX, total_blocks), 0)
    lane = lax.broadcasted_iota(jnp.int32, (N_CTX, total_blocks), 1)
    here = (owner_row == (lane >> 5)) & (jnp.broadcast_to(listed[0:1], lane.shape) == 1)
    place_row = jnp.broadcast_to(place_of[0:1], lane.shape)
    small_lane = lax.broadcasted_iota(jnp.int32, (N_CTX, 128), 1)
    wanted = jnp.zeros((N_CTX, 128), jnp.int32)
    for s in range(CAP):
        chosen = sum_lanes(jnp.where(here & (place_row == s), lane & (per_owner - 1), 0))
        wanted = jnp.where(small_lane == s, chosen, wanted)
    offsets[:, 0, :] = wanted

    pl.semaphore_wait(barrier, N_CTX + 3)


    def ask(rank):
        return pltpu.make_async_remote_copy(
            src_ref=offsets.at[owner_of(me, rank)],
            dst_ref=got.at[rank],
            send_sem=ask_send.at[rank],
            recv_sem=ask_recv.at[rank],
            device_id={"ctx": owner_of(me, rank)},
            device_id_type=MESH,
        )

    order = list(range(N_DIRECT, N_CTX)) + list(range(1, N_DIRECT))
    for rank in order:
        ask(rank).start()
    got[0] = offsets[me]

    row = lax.broadcasted_iota(jnp.int32, (blocks, total_blocks), 0)
    lane = lax.broadcasted_iota(jnp.int32, (blocks, total_blocks), 1)
    places = jnp.broadcast_to(place_of[0:1], lane.shape)
    small_row = lax.broadcasted_iota(jnp.int32, (blocks, 128), 0)
    small_lane = lax.broadcasted_iota(jnp.int32, (blocks, 128), 1)
    for qb in range(steps):
        block = jnp.zeros((blocks, 128), jnp.int32)
        for j in range(blocks):
            block = jnp.where(small_row == j, lists[qb, j], block)
        place = sum_lanes(jnp.where(lane == block[:, 0:1], places, 0))
        own = block == (total_blocks - N_CTX * steps + me * steps + qb)
        own_at = jnp.max(jnp.where(own, small_row * blk, -(1 << 20)), axis=0, keepdims=True)
        rank = rank_of(block >> 5, me)
        entry = jnp.where(small_lane == 0, rank, jnp.where(small_lane == 1, place, own_at))
        table[qb * blocks : (qb + 1) * blocks, :] = entry
    to_picked = pltpu.make_async_copy(table, picked, load_sems.at[4])
    to_picked.start()

    low = lax.broadcasted_iota(jnp.int32, (per_owner, 128), 1) < dr
    for i in range(half_blk):
        at = i // 2 * 128
        first = rope_in[:, at : at + 128].astype(f32)
        second = rope_in[:, half_blk * dr + at : half_blk * dr + at + 128].astype(f32)
        if i % 2:
            first = pltpu.roll(first, dr, 1)
        else:
            second = pltpu.roll(second, dr, 1)
        rope[:, i, :] = jnp.where(low, first, second)

    def to_scalars(rank):
        return pltpu.make_async_copy(got.at[rank], asked.at[rank], ask_local.at[rank])

    far_dy = jnp.where(lax.div(z, 2) == 2, 0, 1)
    far_dx = jnp.where(z < 4, 1 + 2 * lax.div(z, 2), 2)
    far_asker = shifted(me, lax.rem(4 - far_dx, 4), far_dy, lax.rem(z, 2))

    def send(kind, rank):
        if rank >= N_DIRECT:
            src = shared.at[rank - N_DIRECT]
            dst = kv.at[rank, pl.ds(z * share_groups, share_groups)]
        else:
            src, dst = ((direct.at[rank], kv.at[rank]), (ropes.at[rank], rp.at[rank]))[kind]
        return pltpu.make_async_remote_copy(
            src_ref=src,
            dst_ref=dst,
            send_sem=ctx_send.at[kind, rank],
            recv_sem=ctx_recv.at[kind, rank],
            device_id={"ctx": asker_of(me, rank)},
            device_id_type=MESH,
        )

    def send_far_ropes():
        return pltpu.make_async_remote_copy(
            src_ref=far_ropes,
            dst_ref=rp.at[N_DIRECT + z],
            send_sem=ctx_send.at[1, N_DIRECT],
            recv_sem=ctx_recv.at[1, N_DIRECT],
            device_id={"ctx": far_asker},
            device_id_type=MESH,
        )

    for rank in order:
        ask(rank).wait_recv()
        to_scalars(rank).start()
    to_scalars(0).start()
    for rank in range(N_DIRECT, N_CTX):
        to_scalars(rank).wait()
        for i in range(share_groups):
            group = z * share_groups + i
            block = asked[rank, 0, lax.div(group, block_groups)]
            shared[rank - N_DIRECT, i] = latent[block, lax.rem(group, block_groups)]
        send(0, rank).start()
    for s in range(CAP):
        far_ropes[s] = rope[asked[N_DIRECT + z, 0, s]].astype(bf16)
    send_far_ropes().start()
    for rank in list(range(1, N_DIRECT)) + [0]:
        to_scalars(rank).wait()
        for s in range(CAP):
            block = asked[rank, 0, s]
            direct[rank, s * block_groups : (s + 1) * block_groups] = latent[block]
            ropes[rank, s] = rope[block].astype(bf16)
        if rank:
            send(0, rank).start()
            send(1, rank).start()
    own = [
        pltpu.make_async_copy(direct.at[0], kv.at[0], own_sems.at[0]),
        pltpu.make_async_copy(ropes.at[0], rp.at[0], own_sems.at[1]),
    ]
    for copy in own:
        copy.start()


    def ring(direction, step, piece, zz):
        if piece == 2:
            moved = rp.at[N_DIRECT + zz]
        else:
            moved = kv.at[pl.ds(N_DIRECT + 4 * piece, 4), pl.ds(zz * share_groups, share_groups)]
        return pltpu.make_async_remote_copy(
            src_ref=moved,
            dst_ref=moved,
            send_sem=ring_send.at[direction, step, piece],
            recv_sem=ring_recv.at[direction, step, piece],
            device_id={"tp": (right, left)[direction]},
            device_id_type=MESH,
        )

    def pieces(direction, step):
        return (0, 1, 2) if step < 3 else ((0,), (1, 2))[direction]

    def seen_from(direction, step):
        return lax.rem(z + (N_Z - step if direction == 0 else step), N_Z)


    def column(dx):
        return lax.rem(x_core + 2 * dx, 8)

    def move_w(i):
        source = (0, 0, 3, 1, 0, 3, 1, 2)[i]
        rows = pl.ds((i - 2) * half_width, half_width) if i in (2, 3) else pl.ds(0, width)
        peer = other_core if i >= 4 else x_next[i % 2]
        block = w_buf.at[column(source), rows]
        return pltpu.make_async_remote_copy(
            src_ref=block,
            dst_ref=block,
            send_sem=w_send.at[i],
            recv_sem=w_recv.at[i],
            device_id={"ctx": peer},
            device_id_type=MESH,
        )

    for step in range(4):
        for piece in range(3):
            if step == 0:
                if piece == 2:
                    send_far_ropes().wait_recv()
                else:
                    for rank in range(N_DIRECT + 4 * piece, N_DIRECT + 4 * piece + 4):
                        send(0, rank).wait_recv()
            for direction in range(2):
                if step:
                    ring(direction, step - 1, piece, seen_from(direction, step)).wait_recv()
                if piece in pieces(direction, step):
                    ring(direction, step, piece, seen_from(direction, step)).start()
        if step == 0:
            for copy in loads:
                copy.wait()
            lane = lax.broadcasted_iota(jnp.int32, (queries, 128), 1)
            for h in range(heads):
                up = jnp.dot(q_nope[:, h * dn : (h + 1) * dn], w_uk[h], preferred_element_type=f32)
                qbuf[:, h, :, 0:dl] = up.astype(bf16).reshape(-1, blk, dl)
                pair = q_rope[:, h // 2 * 128 : h // 2 * 128 + 128]
                if h % 2:
                    pair = jnp.concatenate([pair[:, 64:], pair[:, :64]], axis=1)
                pair = jnp.where(lane < dr, pair, jnp.zeros_like(pair))
                qbuf[:, h, :, dl : dl + 128] = pair.reshape(-1, blk, 128)
        if step == 0:
            own_w.wait()
            for i in (0, 1, 4):
                move_w(i).start()
    for direction in range(2):
        for piece in pieces(direction, 3):
            ring(direction, 3, piece, seen_from(direction, 4)).wait_recv()
    for copy in own:
        copy.wait()
    for rank in range(1, N_DIRECT):
        send(0, rank).wait_recv()
        send(1, rank).wait_recv()


    log2_scale = mscale_sq / math.sqrt(dn + dr) * math.log2(math.e)

    group = 4

    def send_heads(qb, g):
        rows = pl.ds(pl.multiple_of(qb * blk, blk), blk)
        columns = pl.ds(g * group * dv, group * dv)
        return pltpu.make_async_remote_copy(
            src_ref=heads_out.at[0, rows, columns],
            dst_ref=heads_out.at[1, rows, columns],
            send_sem=head_send.at[qb, g],
            recv_sem=head_recv.at[qb, g],
            device_id={"ctx": opposite},
            device_id_type=MESH,
        )

    def attend(qb, carry):
        lane = lax.broadcasted_iota(jnp.int32, (half_blk, 128), 1)
        for j in range(blocks):
            rank, place = picked[qb * blocks + j, 0], picked[qb * blocks + j, 1]
            for i in range(block_groups):
                first = j * blk + 16 * i
                kbuf[first : first + 16, 0:dl] = kv[rank, place * block_groups + i]
            pair = rp[rank, place]
            swapped = jnp.concatenate([pair[:, 64:], pair[:, :64]], axis=1)
            zero = jnp.zeros_like(pair)
            kbuf[j * blk : j * blk + half_blk, dl : dl + 128] = jnp.where(lane < dr, pair, zero)
            kbuf[j * blk + half_blk : (j + 1) * blk, dl : dl + 128] = jnp.where(
                lane < dr, swapped, zero
            )
        ahead = lax.broadcasted_iota(jnp.int32, (blk, keys), 1) - picked[qb * blocks, 2]
        row = lax.broadcasted_iota(jnp.int32, (blk, keys), 0)
        bias = jnp.where((ahead > row) & (ahead < blk), f32(-1e30), f32(0.0))

        key = kbuf[...]
        value = key[:, 0:dl]
        rows = pl.ds(pl.multiple_of(qb * blk, blk), blk)
        all_scores = []
        for g in range(heads // group):
            query = qbuf[qb, g * group : (g + 1) * group].reshape(group * blk, dl + 128)
            all_scores.append(
                lax.dot_general(query, key, (((1,), (1,)), ((), ())), preferred_element_type=f32)
            )
        for g in range(heads // group):
            first = g * group
            scores = all_scores[g]
            scores = (scores.reshape(group, blk, keys) + bias[None]).reshape(group * blk, keys)
            top = jnp.max(scores, axis=1, keepdims=True)
            raised = jnp.exp2((scores - top) * log2_scale)
            total = jnp.sum(raised, axis=1, keepdims=True)
            mixed = jnp.dot(raised.astype(bf16), value, preferred_element_type=f32)
            mixed = (mixed / total).astype(bf16).reshape(group, blk, dl)
            for i in range(group):
                h = first + i
                heads_out[0, rows, h * dv : (h + 1) * dv] = jnp.dot(
                    mixed[i], w_uv[h], preferred_element_type=f32
                ).astype(bf16)
            send_heads(qb, g).start()

        @pl.when(qb == 0)
        def _():
            move_w(0).wait_recv()
            move_w(1).wait_recv()
            for i in (2, 3, 5, 6):
                move_w(i).start()

        return carry

    to_picked.wait()
    lax.fori_loop(0, steps, attend, 0)
    move_w(2).wait_recv()
    move_w(3).wait_recv()
    move_w(7).start()
    for i in (4, 5, 6, 7):
        move_w(i).wait_recv()


    def compute(dz, side):
        zz = lax.rem(z + dz, N_Z)
        part[side, zz] = lax.dot_general(
            w_buf[zz], heads_out[side], (((1,), (1,)), ((), ())), preferred_element_type=f32
        )

    def half(direction):
        return slice(direction * half_width, (direction + 1) * half_width)

    def pass_on(direction, step, side):
        return pltpu.make_async_remote_copy(
            src_ref=sent.at[direction, step, side],
            dst_ref=arrived.at[direction, step, side],
            send_sem=sum_send.at[direction, step, side],
            recv_sem=sum_recv.at[direction, step, side],
            device_id={"tp": (right, left)[direction]},
            device_id_type=MESH,
        )

    for step in range(N_Z - 1):
        for side in range(2):
            if step == 0 and side == 1:
                for qb in range(steps):
                    for g in range(heads // group):
                        send_heads(qb, g).wait_recv()
            if step < 3:
                compute(N_Z - 1 - step, side)
                compute(1 + step, side)
            elif step < 5:
                compute((4, 0)[step - 3], side)
            for direction in range(2):
                to = lax.rem(z + (N_Z - 1 - step, 1 + step)[direction], N_Z)
                mine = part[side, to, half(direction), :]
                if step:
                    pass_on(direction, step - 1, side).wait_recv()
                    mine = mine + arrived[direction, step - 1, side].astype(f32)
                sent[direction, step, side] = mine.astype(bf16)
                pass_on(direction, step, side).start()

    def total_of(side, direction):
        return part[side, z, half(direction), :] + arrived[direction, N_Z - 2, side].astype(f32)

    is_home = y_lo == y_hi

    def send_last(side, direction):
        slot = jnp.where(is_home, 0, 1) if side else 0
        return pltpu.make_async_remote_copy(
            src_ref=last_sent.at[side, direction],
            dst_ref=last_got.at[slot, direction],
            send_sem=last_send.at[side, direction],
            recv_sem=last_recv.at[slot, direction],
            device_id={"ctx": opposite if side else me, "tp": home},
            device_id_type=MESH,
        )

    def landed(slot, direction):
        return pltpu.make_async_remote_copy(
            src_ref=last_sent.at[slot, direction],
            dst_ref=last_got.at[slot, direction],
            send_sem=last_send.at[slot, direction],
            recv_sem=last_recv.at[slot, direction],
            device_id={"ctx": opposite, "tp": home},
            device_id_type=MESH,
        )

    for direction in range(2):
        pass_on(direction, N_Z - 2, 0).wait_recv()
        last_sent[0, direction] = total_of(0, direction).astype(bf16)

        @pl.when(jnp.logical_not(is_home))
        def _():
            send_last(0, direction).start()

    for direction in range(2):
        pass_on(direction, N_Z - 2, 1).wait_recv()
        last_sent[1, direction] = total_of(1, direction).astype(bf16)
        send_last(1, direction).start()

    @pl.when(jnp.logical_not(is_home))
    def _():
        for direction in range(2):
            landed(0, direction).wait_recv()
            landed(1, direction).wait_recv()
            sum_of_both = last_got[0, direction].astype(f32) + last_got[1, direction].astype(f32)
            out[half(direction), :] = sum_of_both.astype(bf16)
            send_last(0, direction).wait_send()

    @pl.when(is_home)
    def _():
        for direction in range(2):
            landed(0, direction).wait_recv()
            mine = total_of(0, direction) + last_got[0, direction].astype(f32)
            out[half(direction), :] = mine.astype(bf16)

    for rank in range(1, N_CTX):
        ask(rank).wait_send()
        send(0, rank).wait_send()
        if rank < N_DIRECT:
            send(1, rank).wait_send()
    send_far_ropes().wait_send()
    for direction in range(2):
        for step in range(4):
            for piece in pieces(direction, step):
                ring(direction, step, piece, seen_from(direction, step)).wait_send()
        for step in range(N_Z - 1):
            for side in range(2):
                pass_on(direction, step, side).wait_send()
    for i in range(8):
        move_w(i).wait_send()
    for qb in range(steps):
        for g in range(heads // group):
            send_heads(qb, g).wait_send()
    for direction in range(2):
        send_last(1, direction).wait_send()


def layer(lists, latent, rope, q_nope, q_rope, w_uk, w_uv, w_out):
    block_groups = latent.shape[1]
    blk = 16 * block_groups
    half, pair = blk // 2, 2 * rope.shape[1] // blk
    queries = q_nope.shape[0]
    heads, dn, dl = w_uk.shape
    dv = w_uv.shape[2]
    steps, blocks = lists.shape
    width, depth = w_out.shape
    asks = (N_CTX, 8, 128)
    vmem = pl.BlockSpec(memory_space=pltpu.VMEM)
    smem = pl.BlockSpec(memory_space=pltpu.SMEM)
    dma = pltpu.SemaphoreType.DMA
    sums = (2, N_Z - 1, 2, width // 2, queries)
    return pl.pallas_call(
        layer_kernel,
        out_shape=jax.ShapeDtypeStruct((width, queries), bf16),
        in_specs=[smem, vmem, vmem] + [pl.BlockSpec(memory_space=pl.ANY)] * 5,
        out_specs=vmem,
        scratch_shapes=[
            pltpu.VMEM(q_nope.shape, bf16),
            pltpu.VMEM(q_rope.shape, bf16),
            pltpu.VMEM(w_uk.shape, bf16),
            pltpu.VMEM(w_uv.shape, bf16),
            dma((5,)),
            pltpu.VMEM((latent.shape[0], half, pair), f32),
            pltpu.VMEM(asks, jnp.int32),
            pltpu.VMEM((steps * blocks, 128), jnp.int32),
            pltpu.SMEM((steps * blocks, 128), jnp.int32),
            pltpu.VMEM(asks, jnp.int32),
            pltpu.SMEM(asks, jnp.int32),
            pltpu.VMEM((N_DIRECT, CAP * block_groups, 16, dl), bf16),
            pltpu.VMEM((N_CTX - N_DIRECT, CAP * block_groups // N_Z, 16, dl), bf16),
            pltpu.VMEM((N_DIRECT, CAP, half, pair), bf16),
            pltpu.VMEM((CAP, half, pair), bf16),
            pltpu.VMEM((N_CTX, CAP * block_groups, 16, dl), bf16),
            pltpu.VMEM((N_CTX, CAP, half, pair), bf16),
            dma((N_CTX,)),
            dma((N_CTX,)),
            dma((N_CTX,)),
            dma((3,)),
            dma((2, N_CTX)),
            dma((2, N_CTX)),
            dma((2, 4, 3)),
            dma((2, 4, 3)),
            pltpu.VMEM((steps, heads, blk, dl + 128), bf16),
            pltpu.VMEM((blocks * blk, dl + 128), bf16),
            pltpu.VMEM((2, queries, heads * dv), bf16),
            dma((steps, 2)),
            dma((steps, 2)),
            pltpu.VMEM((N_Z, width, depth), bf16),
            dma((8,)),
            dma((8,)),
            pltpu.VMEM((2, N_Z, width, queries), f32),
            pltpu.VMEM(sums, bf16),
            pltpu.VMEM(sums, bf16),
            dma(sums[:3]),
            dma(sums[:3]),
            pltpu.VMEM((2, 2, width // 2, queries), bf16),
            pltpu.VMEM((2, 2, width // 2, queries), bf16),
            dma((2, 2)),
            dma((2, 2)),
        ],
        compiler_params=pltpu.CompilerParams(
            collective_id=2, has_side_effects=True, vmem_limit_bytes=VMEM_LIMIT
        ),
    )(lists, latent, rope, q_nope, q_rope, w_uk, w_uv, w_out)


def per_device(q_nope, q_rope, latent, key_rope, w_uk, w_uv, w_out, block_lists):
    per_owner = key_rope.shape[0]
    latent_blocks = latent.reshape(per_owner, -1, 16, latent.shape[1])
    return layer(
        block_lists, latent_blocks, key_rope, q_nope, q_rope, w_uk, w_uv, w_out.T
    ).T


def solution(mesh):
    placed = (
        P("ctx", "tp"),
        P("ctx", "tp"),
        P("ctx", None),
        P("ctx", None),
        P("tp", None, None),
        P("tp", None, None),
        P("tp", "ctx"),
        P("ctx", None),
    )
    return jax.shard_map(
        per_device, mesh=mesh, in_specs=placed, out_specs=P("ctx", "tp"), check_vma=False
    )
```

profile of v0, /device:TPU:8, one launch (start us, length us, event | category | flops | bytes accessed | tf_op | source)
XLA Modules:
  0.0 132.9 jit_solution(9741263664874993923)
XLA Ops:
  0.0 131.3 %shard_map.82 = bf16[448,256]{1,0:T(8,128)(2,1)} custom-call(s32[4,32]{1,0:T(4,128)} %lists.1, bf16[32,4,16,512]{3,2,1,0:T(8,128)(2,1)} %bitcast.3, bf16[32,4096]{1,0:T(8,128)(2,1)} %rope_in.1, bf16[256,1024]{1,0:T(8,128)(2,1)} %q_nope_in.1, bf16[256,512]{1,0:T(8,128)(2,1)} %q_rope_in.1, bf16[8,128,512]{2,1,0:T(8,128)(2,1)} %w_uk_in.1, ...), custom_call_target="tpu_custom_call" | custom-call | tf_op jit(solution)/shard_map/pallas_call | solution.py:577
  131.3 1.6 %copy.10 = bf16[256,448]{0,1:T(8,128)(2,1)} copy(bf16[256,448]{0,1:T(8,128)(2,1)} %bitcast.4) | data formatting | bytes 458752
where the time goes:
time: 133 us
  Pallas kernels  131 us (98%)
  local copies, waits for them, and re-layouts  1.64 us (1%)
    pallas_call x1, Pallas kernels, layer(): pl.pallas_call(layer_kernel, out_shape=jax.ShapeDtypeStruct((width, queri...  131 us

commit v1 on v0

--- a/solution.py
+++ b/solution.py
@@ -234,10 +234,28 @@
     far_dx = jnp.where(z < 4, 1 + 2 * lax.div(z, 2), 2)
     far_asker = shifted(me, lax.rem(4 - far_dx, 4), far_dy, lax.rem(z, 2))
 
+    first_far = N_DIRECT + 4 * y_lo
+
+    def far_asker_of(i):
+        dx = jnp.where(y_lo == 0, 1 + 2 * (i // 2), 2)
+        dy = jnp.where(y_lo == 0, 1, i // 2)
+        return shifted(me, lax.rem(4 - dx, 4), dy, i % 2)
+
+    def swap_far():
+        moved = kv.at[pl.ds(first_far, 4), pl.ds(z * share_groups, share_groups)]
+        return pltpu.make_async_remote_copy(
+            src_ref=moved,
+            dst_ref=moved,
+            send_sem=ctx_send.at[1, N_DIRECT + 1],
+            recv_sem=ctx_recv.at[1, N_DIRECT + 1],
+            device_id={"tp": across},
+            device_id_type=MESH,
+        )
+
     def send(kind, rank):
         if rank >= N_DIRECT:
             src = shared.at[rank - N_DIRECT]
-            dst = kv.at[rank, pl.ds(z * share_groups, share_groups)]
+            dst = kv.at[first_far + rank - N_DIRECT, pl.ds(z * share_groups, share_groups)]
         else:
             src, dst = ((direct.at[rank], kv.at[rank]), (ropes.at[rank], rp.at[rank]))[kind]
         return pltpu.make_async_remote_copy(
@@ -245,7 +263,7 @@
             dst_ref=dst,
             send_sem=ctx_send.at[kind, rank],
             recv_sem=ctx_recv.at[kind, rank],
-            device_id={"ctx": asker_of(me, rank)},
+            device_id={"ctx": far_asker_of(rank - N_DIRECT) if rank >= N_DIRECT else asker_of(me, rank)},
             device_id_type=MESH,
         )
 
@@ -265,9 +283,10 @@
     to_scalars(0).start()
     for rank in range(N_DIRECT, N_CTX):
         to_scalars(rank).wait()
+    for rank in range(N_DIRECT, N_DIRECT + 4):
         for i in range(share_groups):
             group = z * share_groups + i
-            block = asked[rank, 0, lax.div(group, block_groups)]
+            block = asked[first_far + rank - N_DIRECT, 0, lax.div(group, block_groups)]
             shared[rank - N_DIRECT, i] = latent[block, lax.rem(group, block_groups)]
         send(0, rank).start()
     for s in range(CAP):
@@ -294,7 +313,8 @@
         if piece == 2:
             moved = rp.at[N_DIRECT + zz]
         else:
-            moved = kv.at[pl.ds(N_DIRECT + 4 * piece, 4), pl.ds(zz * share_groups, share_groups)]
+            fetched_by = y_lo if piece == 0 else 1 - y_lo
+            moved = kv.at[pl.ds(N_DIRECT + 4 * fetched_by, 4), pl.ds(zz * share_groups, share_groups)]
         return pltpu.make_async_remote_copy(
             src_ref=moved,
             dst_ref=moved,
@@ -329,13 +349,16 @@
         )
 
     for step in range(4):
-        for piece in range(3):
+        for piece in (0, 2, 1):
             if step == 0:
                 if piece == 2:
                     send_far_ropes().wait_recv()
+                elif piece == 1:
+                    swap_far().wait_recv()
                 else:
-                    for rank in range(N_DIRECT + 4 * piece, N_DIRECT + 4 * piece + 4):
+                    for rank in range(N_DIRECT, N_DIRECT + 4):
                         send(0, rank).wait_recv()
+                    swap_far().start()
             for direction in range(2):
                 if step:
                     ring(direction, step - 1, piece, seen_from(direction, step)).wait_recv()
@@ -540,10 +563,12 @@
 
     for rank in range(1, N_CTX):
         ask(rank).wait_send()
-        send(0, rank).wait_send()
+        if rank < N_DIRECT + 4:
+            send(0, rank).wait_send()
         if rank < N_DIRECT:
             send(1, rank).wait_send()
     send_far_ropes().wait_send()
+    swap_far().wait_send()
     for direction in range(2):
         for step in range(4):
             for piece in pieces(direction, step):
@@ -592,7 +617,7 @@
             pltpu.VMEM(asks, jnp.int32),
             pltpu.SMEM(asks, jnp.int32),
             pltpu.VMEM((N_DIRECT, CAP * block_groups, 16, dl), bf16),
-            pltpu.VMEM((N_CTX - N_DIRECT, CAP * block_groups // N_Z, 16, dl), bf16),
+            pltpu.VMEM((4, CAP * block_groups // N_Z, 16, dl), bf16),
             pltpu.VMEM((N_DIRECT, CAP, half, pair), bf16),
             pltpu.VMEM((CAP, half, pair), bf16),
             pltpu.VMEM((N_CTX, CAP * block_groups, 16, dl), bf16),

time: 133 us -> 146 us (1.098)
  Pallas kernels: 131 us -> 144 us
    pallas_call x1, Pallas kernels: 131 us -> 144 us  [layer(): pl.pallas_call(layer_kernel, out_shape=jax.ShapeDtypeStruct((width, queri...]
where the time goes in v1:
time: 146 us
  Pallas kernels  144 us (99%)
  local copies, waits for them, and re-layouts  1.64 us (1%)
    pallas_call x1, Pallas kernels, layer(): pl.pallas_call(layer_kernel, out_shape=jax.ShapeDtypeStruct((width, queri...  144 us

profile of v1, /device:TPU:8, one launch (start us, length us, event | category | flops | bytes accessed | tf_op | source)
XLA Modules:
  0.0 146.1 jit_solution(8817989751288666778)
XLA Ops:
  0.0 144.5 %shard_map.82 = bf16[448,256]{1,0:T(8,128)(2,1)} custom-call(s32[4,32]{1,0:T(4,128)} %lists.1, bf16[32,4,16,512]{3,2,1,0:T(8,128)(2,1)} %bitcast.3, bf16[32,4096]{1,0:T(8,128)(2,1)} %rope_in.1, bf16[256,1024]{1,0:T(8,128)(2,1)} %q_nope_in.1, bf16[256,512]{1,0:T(8,128)(2,1)} %q_rope_in.1, bf16[8,128,512]{2,1,0:T(8,128)(2,1)} %w_uk_in.1, ...), custom_call_target="tpu_custom_call" | custom-call | tf_op jit(solution)/shard_map/pallas_call | solution.py:602
  144.5 1.6 %copy.10 = bf16[256,448]{0,1:T(8,128)(2,1)} copy(bf16[256,448]{0,1:T(8,128)(2,1)} %bitcast.4) | data formatting | bytes 458752

commit v2 on v0

--- a/solution.py
+++ b/solution.py
@@ -53,14 +53,16 @@
 
 def layer_kernel(
     lists,
-    latent,
-    rope_in,
+    latent_in,
+    rope_flat,
     q_nope_in,
     q_rope_in,
     w_uk_in,
     w_uv_in,
     w_out,
     out,
+    latent,
+    rope_in,
     q_nope,
     q_rope,
     w_uk,
@@ -147,7 +149,7 @@
     loads = [
         pltpu.make_async_copy(src, dst, load_sems.at[i])
         for i, (src, dst) in enumerate(
-            ((q_nope_in, q_nope), (q_rope_in, q_rope), (w_uk_in, w_uk), (w_uv_in, w_uv))
+            ((latent_in, latent), (rope_flat, rope_in), (q_nope_in, q_nope), (q_rope_in, q_rope), (w_uk_in, w_uk), (w_uv_in, w_uv))
         )
     ]
     for copy in loads:
@@ -198,24 +200,52 @@
         ask(rank).start()
     got[0] = offsets[me]
 
-    row = lax.broadcasted_iota(jnp.int32, (blocks, total_blocks), 0)
-    lane = lax.broadcasted_iota(jnp.int32, (blocks, total_blocks), 1)
-    places = jnp.broadcast_to(place_of[0:1], lane.shape)
-    small_row = lax.broadcasted_iota(jnp.int32, (blocks, 128), 0)
-    small_lane = lax.broadcasted_iota(jnp.int32, (blocks, 128), 1)
-    for qb in range(steps):
-        block = jnp.zeros((blocks, 128), jnp.int32)
-        for j in range(blocks):
-            block = jnp.where(small_row == j, lists[qb, j], block)
-        place = sum_lanes(jnp.where(lane == block[:, 0:1], places, 0))
-        own = block == (total_blocks - N_CTX * steps + me * steps + qb)
-        own_at = jnp.max(jnp.where(own, small_row * blk, -(1 << 20)), axis=0, keepdims=True)
-        rank = rank_of(block >> 5, me)
-        entry = jnp.where(small_lane == 0, rank, jnp.where(small_lane == 1, place, own_at))
-        table[qb * blocks : (qb + 1) * blocks, :] = entry
-    to_picked = pltpu.make_async_copy(table, picked, load_sems.at[4])
-    to_picked.start()
-
+
+    def to_scalars(rank):
+        return pltpu.make_async_copy(got.at[rank], asked.at[rank], ask_local.at[rank])
+
+    far_dy = jnp.where(lax.div(z, 2) == 2, 0, 1)
+    far_dx = jnp.where(z < 4, 1 + 2 * lax.div(z, 2), 2)
+    far_asker = shifted(me, lax.rem(4 - far_dx, 4), far_dy, lax.rem(z, 2))
+
+    def send(kind, rank):
+        if rank >= N_DIRECT:
+            src = shared.at[rank - N_DIRECT]
+            dst = kv.at[rank, pl.ds(z * share_groups, share_groups)]
+        else:
+            src, dst = ((direct.at[rank], kv.at[rank]), (ropes.at[rank], rp.at[rank]))[kind]
+        return pltpu.make_async_remote_copy(
+            src_ref=src,
+            dst_ref=dst,
+            send_sem=ctx_send.at[kind, rank],
+            recv_sem=ctx_recv.at[kind, rank],
+            device_id={"ctx": asker_of(me, rank)},
+            device_id_type=MESH,
+        )
+
+    def send_far_ropes():
+        return pltpu.make_async_remote_copy(
+            src_ref=far_ropes,
+            dst_ref=rp.at[N_DIRECT + z],
+            send_sem=ctx_send.at[1, N_DIRECT],
+            recv_sem=ctx_recv.at[1, N_DIRECT],
+            device_id={"ctx": far_asker},
+            device_id_type=MESH,
+        )
+
+    for rank in order:
+        ask(rank).wait_recv()
+        to_scalars(rank).start()
+    to_scalars(0).start()
+    loads[0].wait()
+    for rank in range(N_DIRECT, N_CTX):
+        to_scalars(rank).wait()
+        for i in range(share_groups):
+            group = z * share_groups + i
+            block = asked[rank, 0, lax.div(group, block_groups)]
+            shared[rank - N_DIRECT, i] = latent[block, lax.rem(group, block_groups)]
+        send(0, rank).start()
+    loads[1].wait()
     low = lax.broadcasted_iota(jnp.int32, (per_owner, 128), 1) < dr
     for i in range(half_blk):
         at = i // 2 * 128
@@ -227,49 +257,6 @@
             second = pltpu.roll(second, dr, 1)
         rope[:, i, :] = jnp.where(low, first, second)
 
-    def to_scalars(rank):
-        return pltpu.make_async_copy(got.at[rank], asked.at[rank], ask_local.at[rank])
-
-    far_dy = jnp.where(lax.div(z, 2) == 2, 0, 1)
-    far_dx = jnp.where(z < 4, 1 + 2 * lax.div(z, 2), 2)
-    far_asker = shifted(me, lax.rem(4 - far_dx, 4), far_dy, lax.rem(z, 2))
-
-    def send(kind, rank):
-        if rank >= N_DIRECT:
-            src = shared.at[rank - N_DIRECT]
-            dst = kv.at[rank, pl.ds(z * share_groups, share_groups)]
-        else:
-            src, dst = ((direct.at[rank], kv.at[rank]), (ropes.at[rank], rp.at[rank]))[kind]
-        return pltpu.make_async_remote_copy(
-            src_ref=src,
-            dst_ref=dst,
-            send_sem=ctx_send.at[kind, rank],
-            recv_sem=ctx_recv.at[kind, rank],
-            device_id={"ctx": asker_of(me, rank)},
-            device_id_type=MESH,
-        )
-
-    def send_far_ropes():
-        return pltpu.make_async_remote_copy(
-            src_ref=far_ropes,
-            dst_ref=rp.at[N_DIRECT + z],
-            send_sem=ctx_send.at[1, N_DIRECT],
-            recv_sem=ctx_recv.at[1, N_DIRECT],
-            device_id={"ctx": far_asker},
-            device_id_type=MESH,
-        )
-
-    for rank in order:
-        ask(rank).wait_recv()
-        to_scalars(rank).start()
-    to_scalars(0).start()
-    for rank in range(N_DIRECT, N_CTX):
-        to_scalars(rank).wait()
-        for i in range(share_groups):
-            group = z * share_groups + i
-            block = asked[rank, 0, lax.div(group, block_groups)]
-            shared[rank - N_DIRECT, i] = latent[block, lax.rem(group, block_groups)]
-        send(0, rank).start()
     for s in range(CAP):
         far_ropes[s] = rope[asked[N_DIRECT + z, 0, s]].astype(bf16)
     send_far_ropes().start()
@@ -342,7 +329,24 @@
                 if piece in pieces(direction, step):
                     ring(direction, step, piece, seen_from(direction, step)).start()
         if step == 0:
-            for copy in loads:
+            row = lax.broadcasted_iota(jnp.int32, (blocks, total_blocks), 0)
+            key_lane = lax.broadcasted_iota(jnp.int32, (blocks, total_blocks), 1)
+            places = jnp.broadcast_to(place_of[0:1], key_lane.shape)
+            small_row = lax.broadcasted_iota(jnp.int32, (blocks, 128), 0)
+            small_lane = lax.broadcasted_iota(jnp.int32, (blocks, 128), 1)
+            for qb in range(steps):
+                block = jnp.zeros((blocks, 128), jnp.int32)
+                for j in range(blocks):
+                    block = jnp.where(small_row == j, lists[qb, j], block)
+                place = sum_lanes(jnp.where(key_lane == block[:, 0:1], places, 0))
+                is_own = block == (total_blocks - N_CTX * steps + me * steps + qb)
+                own_at = jnp.max(jnp.where(is_own, small_row * blk, -(1 << 20)), axis=0, keepdims=True)
+                rank = rank_of(block >> 5, me)
+                entry = jnp.where(small_lane == 0, rank, jnp.where(small_lane == 1, place, own_at))
+                table[qb * blocks : (qb + 1) * blocks, :] = entry
+            to_picked = pltpu.make_async_copy(table, picked, load_sems.at[6])
+            to_picked.start()
+            for copy in loads[2:]:
                 copy.wait()
             lane = lax.broadcasted_iota(jnp.int32, (queries, 128), 1)
             for h in range(heads):
@@ -577,14 +581,16 @@
     return pl.pallas_call(
         layer_kernel,
         out_shape=jax.ShapeDtypeStruct((width, queries), bf16),
-        in_specs=[smem, vmem, vmem] + [pl.BlockSpec(memory_space=pl.ANY)] * 5,
+        in_specs=[smem] + [pl.BlockSpec(memory_space=pl.ANY)] * 7,
         out_specs=vmem,
         scratch_shapes=[
+            pltpu.VMEM(latent.shape, bf16),
+            pltpu.VMEM(rope.shape, bf16),
             pltpu.VMEM(q_nope.shape, bf16),
             pltpu.VMEM(q_rope.shape, bf16),
             pltpu.VMEM(w_uk.shape, bf16),
             pltpu.VMEM(w_uv.shape, bf16),
-            dma((5,)),
+            dma((7,)),
             pltpu.VMEM((latent.shape[0], half, pair), f32),
             pltpu.VMEM(asks, jnp.int32),
             pltpu.VMEM((steps * blocks, 128), jnp.int32),

time: 133 us -> 132 us (level)
  no operation moved by 1% of the time
where the time goes in v2:
time: 132 us
  Pallas kernels  130 us (98%)
  local copies, waits for them, and re-layouts  1.64 us (1%)
    pallas_call x1, Pallas kernels, layer(): pl.pallas_call(layer_kernel, out_shape=jax.ShapeDtypeStruct((width, queri...  130 us

profile of v2, /device:TPU:8, one launch (start us, length us, event | category | flops | bytes accessed | tf_op | source)
XLA Modules:
  0.0 132.0 jit_solution(11160346853035484796)
XLA Ops:
  0.0 130.4 %shard_map.82 = bf16[448,256]{1,0:T(8,128)(2,1)} custom-call(s32[4,32]{1,0:T(4,128)} %lists.1, bf16[32,4,16,512]{3,2,1,0:T(8,128)(2,1)} %bitcast.3, bf16[32,4096]{1,0:T(8,128)(2,1)} %rope_flat.1, bf16[256,1024]{1,0:T(8,128)(2,1)} %q_nope_in.1, bf16[256,512]{1,0:T(8,128)(2,1)} %q_rope_in.1, bf16[8,128,512]{2,1,0:T(8,128)(2,1)} %w_uk_in.1, ...), custom_call_target="tpu_custom_call" | custom-call | tf_op jit(solution)/shard_map/pallas_call | solution.py:581
  130.4 1.6 %copy.10 = bf16[256,448]{0,1:T(8,128)(2,1)} copy(bf16[256,448]{0,1:T(8,128)(2,1)} %bitcast.4) | data formatting | bytes 458752

commit v3 on v2

--- a/solution.py
+++ b/solution.py
@@ -329,6 +329,9 @@
                 if piece in pieces(direction, step):
                     ring(direction, step, piece, seen_from(direction, step)).start()
         if step == 0:
+            own_w.wait()
+            for i in (0, 1, 4):
+                move_w(i).start()
             row = lax.broadcasted_iota(jnp.int32, (blocks, total_blocks), 0)
             key_lane = lax.broadcasted_iota(jnp.int32, (blocks, total_blocks), 1)
             places = jnp.broadcast_to(place_of[0:1], key_lane.shape)
@@ -357,10 +360,6 @@
                     pair = jnp.concatenate([pair[:, 64:], pair[:, :64]], axis=1)
                 pair = jnp.where(lane < dr, pair, jnp.zeros_like(pair))
                 qbuf[:, h, :, dl : dl + 128] = pair.reshape(-1, blk, 128)
-        if step == 0:
-            own_w.wait()
-            for i in (0, 1, 4):
-                move_w(i).start()
     for direction in range(2):
         for piece in pieces(direction, 3):
             ring(direction, 3, piece, seen_from(direction, 4)).wait_recv()

time: 132 us -> 132 us (level)
  no operation moved by 1% of the time
where the time goes in v3:
time: 132 us
  Pallas kernels  130 us (98%)
  local copies, waits for them, and re-layouts  1.64 us (1%)
    pallas_call x1, Pallas kernels, layer(): pl.pallas_call(layer_kernel, out_shape=jax.ShapeDtypeStruct((width, queri...  130 us

profile of v3, /device:TPU:8, one launch (start us, length us, event | category | flops | bytes accessed | tf_op | source)
XLA Modules:
  0.0 132.0 jit_solution(15239212024953108942)
XLA Ops:
  0.0 130.4 %shard_map.82 = bf16[448,256]{1,0:T(8,128)(2,1)} custom-call(s32[4,32]{1,0:T(4,128)} %lists.1, bf16[32,4,16,512]{3,2,1,0:T(8,128)(2,1)} %bitcast.3, bf16[32,4096]{1,0:T(8,128)(2,1)} %rope_flat.1, bf16[256,1024]{1,0:T(8,128)(2,1)} %q_nope_in.1, bf16[256,512]{1,0:T(8,128)(2,1)} %q_rope_in.1, bf16[8,128,512]{2,1,0:T(8,128)(2,1)} %w_uk_in.1, ...), custom_call_target="tpu_custom_call" | custom-call | tf_op jit(solution)/shard_map/pallas_call | solution.py:580
  130.4 1.6 %copy.10 = bf16[256,448]{0,1:T(8,128)(2,1)} copy(bf16[256,448]{0,1:T(8,128)(2,1)} %bitcast.4) | data formatting | bytes 458752
